TPU v7x, 32 devices: a whole 2x2x4 slice. The times are simulated.
32 devices in a mesh: groups: 2 (over x), tm: 16 (over z, y, core).
Axes of the slice: x: 2, y: 2, z: 4, core: 2. Of those that a mesh axis runs over, the one named last changes fastest.
Arguments:
- tokens: bfloat16 [2, 4096, 1152], P('groups', 'tm'), parts along dimension 0, may hold values from -6 to 6
- norm_gain: float32 [1152], replicated, may hold values from 0.5 to 8
- w_qkv: bfloat16 [1152, 1728], P('tm'), may hold values from -0.1875 to 0.1875
- w_out: bfloat16 [1152, 576], P('tm'), may hold values from -0.25 to 0.25
- block_mask: int32 [2, 2, 2], P('groups'), parts along dimension 0, may hold values from 0 to 1
- keep_tiles: int32 [2, 256], P('groups', 'tm'), parts along dimension 0, may hold values 0 or 1
- cotangent: bfloat16 [2, 4096, 1152], P('groups', 'tm'), parts along dimension 0, may hold values from -6 to 6
Outputs:
- mixed: bfloat16 [2, 4096, 1152], P('groups', 'tm'), parts along dimension 0
- grad_tokens: bfloat16 [2, 4096, 1152], P('groups', 'tm'), parts along dimension 0
- grad_qkv: float32 [2304, 1728], P(('groups', 'tm')), parts along dimension 0
- grad_out: float32 [2304, 576], P(('groups', 'tm')), parts along dimension 0
There are 2 independent parts, one for each index of `groups`. A program takes and returns all parts, laid end to end along the dimension named above; an argument that names none is the same for every part. Nothing has to cross between parts.
All inputs are finite; a program needn't handle non-finite values. No bound on the sum of `keep_tiles` on one device may be relied on, other than what follows from the above.
Results may differ from a plain program's by a relative error of at most 0.0055.
The roundings to bfloat16 on the way count: a program that leaves them out, or rounds other values in their place, can miss the bound.
Values may be sent and summed in bfloat16 or wider, within the bound.
A program may use at most 128 MiB of HBM per device.

v0:
```python
import jax
import jax.numpy as jnp
from jax import lax
from jax.sharding import PartitionSpec as P

HD = 72
SPLIT = 4
TB = 2
TILE = 16
EPS = 1e-06


def temporal(qkv_cols, dattn_cols, keep_cols, block_mask, frames):
    videos, per_owner, owners, _ = qkv_cols.shape
    band_count = owners // frames
    heads_n = dattn_cols.shape[-1] // HD
    scale = HD ** (-0.5)
    parts = qkv_cols.reshape(videos, per_owner, frames, band_count, 3, heads_n, HD)
    queries = parts[:, :, :, :, 0]
    key_part = parts[:, :, :, :, 1]
    val_part = parts[:, :, :, :, 2]
    d_out = dattn_cols.reshape(videos, per_owner, frames, band_count, heads_n, HD)
    frame_block = jnp.arange(frames) // TB
    blocks = jnp.repeat(jnp.repeat(block_mask, TB, 1), TB, 2) > 0
    same_block = frame_block[:, None] == frame_block[None, :]
    block_allow = blocks | same_block[None]
    kept = jnp.transpose(keep_cols.reshape(videos, per_owner, frames, band_count) > 0, (0, 1, 3, 2))
    diag_one = jnp.arange(frames)[:, None] == jnp.arange(frames)[None, :]
    allow = block_allow[:, None, None, None, :, :] & (kept[:, :, :, None, None, :] | diag_one)
    scores = (
        jnp.einsum("vrfshd,vrgshd->vrshfg", queries, key_part, preferred_element_type=jnp.float32)
        * scale
    )
    scores = jnp.where(allow, scores, -1e30)
    row_top = jnp.max(scores, -1, keepdims=True)
    expo = jnp.exp(scores - row_top)
    probs = expo / jnp.sum(expo, -1, keepdims=True)
    probs_b = probs.astype(jnp.bfloat16)
    attn = jnp.einsum(
        "vrshfg,vrgshd->vrfshd", probs_b, val_part, preferred_element_type=jnp.float32
    ).astype(jnp.bfloat16)
    dprob = jnp.einsum("vrfshd,vrgshd->vrshfg", d_out, val_part, preferred_element_type=jnp.float32)
    dscore = probs * (dprob - jnp.sum(probs * dprob, -1, keepdims=True))
    dscore_b = dscore.astype(jnp.bfloat16)
    grad_query = (
        jnp.einsum("vrshfg,vrgshd->vrfshd", dscore_b, key_part, preferred_element_type=jnp.float32)
        * scale
    ).astype(jnp.bfloat16)
    grad_key = (
        jnp.einsum("vrshfg,vrfshd->vrgshd", dscore_b, queries, preferred_element_type=jnp.float32)
        * scale
    ).astype(jnp.bfloat16)
    grad_value = jnp.einsum(
        "vrshfg,vrfshd->vrgshd", probs_b, d_out, preferred_element_type=jnp.float32
    ).astype(jnp.bfloat16)
    d_qkv = jnp.stack([grad_query, grad_key, grad_value], axis=4).reshape(
        videos, per_owner, owners, -1
    )
    return (attn.reshape(videos, per_owner, owners, -1), d_qkv)


def per_device(tokens, norm_gain, w_qkv, w_out, block_mask, keep_tiles, cotangent):
    owners = lax.axis_size("tm")
    videos, band_len, model_width = tokens.shape
    per_owner = band_len // owners
    frames = owners // SPLIT
    qkv_full, out_full = (
        lax.all_gather(w_qkv, "tm", axis=0, tiled=True),
        lax.all_gather(w_out, "tm", axis=0, tiled=True),
    )
    tok_float = tokens.astype(jnp.float32)
    inv_rms = lax.rsqrt(jnp.mean(tok_float * tok_float, -1, keepdims=True) + EPS)
    normed = tok_float * inv_rms
    hidden = (normed * norm_gain).astype(jnp.bfloat16)
    keep_tok = jnp.repeat(keep_tiles, TILE, axis=1).reshape(videos, per_owner, owners)
    qkv = jnp.dot(hidden, qkv_full, preferred_element_type=jnp.float32).astype(jnp.bfloat16)
    d_attn = jnp.dot(cotangent, out_full, preferred_element_type=jnp.float32).astype(jnp.bfloat16)
    qkv_cols, dattn_cols, keep_cols = (
        lax.all_to_all(
            qkv.reshape(videos, per_owner, owners, -1),
            "tm",
            split_axis=2,
            concat_axis=2,
            tiled=True,
        ),
        lax.all_to_all(
            d_attn.reshape(videos, per_owner, owners, -1),
            "tm",
            split_axis=2,
            concat_axis=2,
            tiled=True,
        ),
        lax.all_to_all(keep_tok, "tm", split_axis=2, concat_axis=2, tiled=True),
    )
    attn_cols, dqkv_cols = temporal(qkv_cols, dattn_cols, keep_cols, block_mask, frames)
    attn_rows, dqkv_rows = (
        lax.all_to_all(attn_cols, "tm", split_axis=2, concat_axis=2, tiled=True),
        lax.all_to_all(dqkv_cols, "tm", split_axis=2, concat_axis=2, tiled=True),
    )
    attn = attn_rows.reshape(videos, band_len, -1)
    d_qkv = dqkv_rows.reshape(videos, band_len, -1)
    part_qkv = jnp.einsum("vtd,vte->de", hidden, d_qkv, preferred_element_type=jnp.float32)
    part_out = jnp.einsum("vtd,vte->de", cotangent, attn, preferred_element_type=jnp.float32)
    d_hidden = lax.optimization_barrier(
        jnp.einsum("vte,de->vtd", d_qkv, qkv_full, preferred_element_type=jnp.float32).astype(
            jnp.bfloat16
        )
    )
    grad_qkv, grad_out = (
        lax.psum_scatter(part_qkv, "tm", scatter_dimension=0, tiled=True),
        lax.psum_scatter(part_out, "tm", scatter_dimension=0, tiled=True),
    )
    mixed = (
        tok_float + jnp.einsum("vte,de->vtd", attn, out_full, preferred_element_type=jnp.float32)
    ).astype(jnp.bfloat16)
    grad = d_hidden.astype(jnp.float32) * norm_gain
    grad_tokens = cotangent.astype(jnp.float32) + inv_rms * (
        grad - normed * jnp.mean(grad * normed, -1, keepdims=True)
    )
    return (mixed, grad_tokens.astype(jnp.bfloat16), grad_qkv, grad_out)


def solution(mesh):
    placed = (
        P("groups", "tm", None),
        P(),
        P("tm", None),
        P("tm", None),
        P("groups", None, None),
        P("groups", "tm"),
        P("groups", "tm", None),
    )
    return jax.shard_map(
        per_device,
        mesh=mesh,
        in_specs=placed,
        out_specs=(
            P("groups", "tm", None),
            P("groups", "tm", None),
            P(("groups", "tm"), None),
            P(("groups", "tm"), None),
        ),
        check_vma=False,
    )
```

profile of v0, /device:TPU:0, one launch (start us, length us, event | category | flops | bytes accessed | tf_op | source)
XLA Modules:
  0.0 400.1 jit_solution(6253478221850050072)
XLA Ops:
  9.9 7.4 %all-to-all-start.1 = ((s32[1,16,16]{1,0,2:T(1,128)}), s32[1,16,16]{1,0,2:T(1,128)S(1)}, u32[]{:S(2)}, u32[]{:S(2)}) async-start(s32[1,16,16]{1,0,2:T(1,128)} %broadcast_in_dim.16), calls=%async_computation.1 | async-start | bytes 16384 | tf_op jit(solution)/shard_map/all_to_all | solution.py:93
  18.6 33.7 %all-gather.5.cloned.1.call-done = bf16[1152,576]{1,0:T(8,128)(2,1)} async-done(((bf16[72,576]{1,0:T(8,128)(2,1)}), bf16[1152,576]{1,0:T(8,128)(2,1)}) %all-gather.5.cloned.1.call-update) | async-done | bytes 1327120 | tf_op jit(solution)/shard_map/all_gather | solution.py:69
  52.2 2.3 convolution_convert_fusion.4
  55.5 3.5 all-to-all-start.3
  59.1 48.6 %all-gather.3.cloned.1.call-done = bf16[1152,1728]{1,0:T(8,128)(2,1)} async-done(((bf16[72,1728]{1,0:T(8,128)(2,1)}), bf16[1152,1728]{1,0:T(8,128)(2,1)}) %all-gather.3.cloned.1.call-update) | async-done | bytes 3981328 | tf_op jit(solution)/shard_map/all_gather | solution.py:68
  107.7 4.0 convolution_convert_fusion.1
  113.6 3.9 all-to-all-start
  120.1 18.1 %all-to-all-done = bf16[1,16,16,1728]{3,1,0,2:T(8,128)(2,1)S(1)} async-done(((bf16[1,16,16,1728]{3,1,0,2:T(8,128)(2,1)}), bf16[1,16,16,1728]{3,1,0,2:T(8,128)(2,1)S(1)}, u32[]{:S(2)}, u32[]{:S(2)}) %all-to-all-start) | async-done | bytes 884768 | tf_op jit(solution)/shard_map/all_to_all | solution.py:79
  138.2 1.7 reshape.294
  141.4 3.1 fusion.35
  148.8 1.7 fusion.13
  151.7 6.1 %all-to-all-start.2 = ((bf16[1,16,16,576]{3,1,0,2:T(8,128)(2,1)}), bf16[1,16,16,576]{3,1,0,2:T(8,128)(2,1)S(1)}, u32[]{:S(2)}, u32[]{:S(2)}) async-start(bf16[1,16,16,576]{3,1,0,2:T(8,128)(2,1)} %reshape.289), calls=%async_computation.2 | async-start | bytes 655360 | tf_op jit(solution)/shard_map/all_to_all | solution.py:97
  157.8 1.8 fusion.15
  159.6 1.5 pad_maximum_fusion
  161.4 1.9 reshape.290
  163.3 5.6 %all-to-all-done.2 = bf16[1,16,16,576]{3,1,0,2:T(8,128)(2,1)S(1)} async-done(((bf16[1,16,16,576]{3,1,0,2:T(8,128)(2,1)}), bf16[1,16,16,576]{3,1,0,2:T(8,128)(2,1)S(1)}, u32[]{:S(2)}, u32[]{:S(2)}) %all-to-all-start.2) | async-done | bytes 294944 | tf_op jit(solution)/shard_map/all_to_all | solution.py:97
  168.9 3.6 all-to-all-start.4
  172.7 2.0 convolution_bitcast_fusion
  174.8 23.5 %all-to-all-done.4 = bf16[1,16,16,1728]{3,1,0,2:T(8,128)(2,1)S(1)} async-done(((bf16[1,16,16,1728]{3,1,0,2:T(8,128)(2,1)}), bf16[1,16,16,1728]{3,1,0,2:T(8,128)(2,1)S(1)}, u32[]{:S(2)}, u32[]{:S(2)}) %all-to-all-start.4) | async-done | bytes 884768 | tf_op jit(solution)/shard_map/all_to_all | solution.py:98
  199.5 4.6 %fusion.31 = f32[1152,1728]{1,0:T(8,128)} fusion(bf16[256,1728]{1,0:T(8,128)(2,1)S(1)} %bitcast.103, bf16[1,256,1152]{2,1,0:T(8,128)(2,1)S(1)} %copy-done, f32[1152]{0:T(1024)S(1)} %copy-done.10, f32[256]{0:T(256)S(1)} %add_rsqrt_fusion), kind=kOutput, calls=%fused_computation.51 | convolution fusion | flops 1020395520 | bytes 9442816 | tf_op jit(solution)/shard_map/vtd,vte->de/dot_general | solution.py:102
  206.0 1.5 fusion.2
  207.5 3.6 fusion.3
  212.7 73.5 %all-reduce.3.cloned.1.call-done = f32[1152,576]{0,1:T(8,128)} async-done(((f32[1152,576]{0,1:T(8,128)}), f32[1152,576]{0,1:T(8,128)}) %all-reduce.3.cloned.1.call-update) | async-done | bytes 2654224
  288.2 105.4 %reduce-scatter.3.cloned.1.call-done = f32[72,1728]{1,0:T(8,128)} async-done(((f32[1152,1728]{1,0:T(8,128)}), f32[72,1728]{1,0:T(8,128)}) %reduce-scatter.3.cloned.1.call-update) | async-done | bytes 497680 | tf_op jit(solution)/shard_map/reduce_scatter | solution.py:110
  (71 shorter events, 22.8 us)
Async XLA Ops:
  7.2 45.1 %all-gather.5.cloned.1.call-start = ((), (), s32[]{:S(2)}) async-start(), calls=%async_computation.7 | async-start | bytes 1566720 | tf_op jit(solution)/shard_map/all_gather | solution.py:69
  7.9 99.8 %all-gather.3.cloned.1.call-start = ((), (), s32[]{:S(2)}) async-start(), calls=%async_computation.6 | async-start | bytes 4386816 | tf_op jit(solution)/shard_map/all_gather | solution.py:68
  9.9 45.6 %all-to-all-start.1 = ((s32[1,16,16]{1,0,2:T(1,128)}), s32[1,16,16]{1,0,2:T(1,128)S(1)}, u32[]{:S(2)}, u32[]{:S(2)}) async-start(s32[1,16,16]{1,0,2:T(1,128)} %broadcast_in_dim.16), calls=%async_computation.1 | async-start | bytes 16384 | tf_op jit(solution)/shard_map/all_to_all | solution.py:93
  54.5 53.2 %copy-start = (bf16[1,256,1152]{2,1,0:T(8,128)(2,1)S(1)}, bf16[1,256,1152]{2,1,0:T(8,128)(2,1)}, u32[]{:S(2)}) copy-start(bf16[1,256,1152]{2,1,0:T(8,128)(2,1)} %param.7) | copy-start | bytes 1769476
  54.5 53.2 %copy-start.10 = (f32[1152]{0:T(1024)S(1)}, f32[1152]{0:T(1024)}, u32[]{:S(2)}) copy-start(f32[1152]{0:T(1024)} %param.8) | copy-start | bytes 13828
  55.5 58.1 %all-to-all-start.3 = ((bf16[1,16,16,576]{3,1,0,2:T(8,128)(2,1)}), bf16[1,16,16,576]{3,1,0,2:T(8,128)(2,1)S(1)}, u32[]{:S(2)}, u32[]{:S(2)}) async-start(bf16[1,16,16,576]{3,1,0,2:T(8,128)(2,1)} %copy.64), calls=%async_computation.3 | async-start | bytes 655360 | tf_op jit(solution)/shard_map/all_to_all | solution.py:86
  113.6 4.0 copy-start.11
  113.6 24.5 %all-to-all-start = ((bf16[1,16,16,1728]{3,1,0,2:T(8,128)(2,1)}), bf16[1,16,16,1728]{3,1,0,2:T(8,128)(2,1)S(1)}, u32[]{:S(2)}, u32[]{:S(2)}) async-start(bf16[1,16,16,1728]{3,1,0,2:T(8,128)(2,1)} %copy.51), calls=%async_computation | async-start | bytes 1835008 | tf_op jit(solution)/shard_map/all_to_all | solution.py:79
  141.4 3.1 copy-start.8
  144.4 2.6 copy-start.9
  144.4 1.1 copy-start.5
  147.0 1.0 copy-start.6
  151.7 17.2 %all-to-all-start.2 = ((bf16[1,16,16,576]{3,1,0,2:T(8,128)(2,1)}), bf16[1,16,16,576]{3,1,0,2:T(8,128)(2,1)S(1)}, u32[]{:S(2)}, u32[]{:S(2)}) async-start(bf16[1,16,16,576]{3,1,0,2:T(8,128)(2,1)} %reshape.289), calls=%async_computation.2 | async-start | bytes 655360 | tf_op jit(solution)/shard_map/all_to_all | solution.py:97
  157.8 1.8 copy-start.7
  163.3 9.4 %copy-start.2 = (bf16[1,256,1152]{2,1,0:T(8,128)(2,1)S(1)}, bf16[1,256,1152]{2,1,0:T(8,128)(2,1)}, u32[]{:S(2)}) copy-start(bf16[1,256,1152]{2,1,0:T(8,128)(2,1)} %param.13) | copy-start | bytes 1769476
  168.9 29.4 %all-to-all-start.4 = ((bf16[1,16,16,1728]{3,1,0,2:T(8,128)(2,1)}), bf16[1,16,16,1728]{3,1,0,2:T(8,128)(2,1)S(1)}, u32[]{:S(2)}, u32[]{:S(2)}) async-start(bf16[1,16,16,1728]{3,1,0,2:T(8,128)(2,1)} %reshape.290), calls=%async_computation.4 | async-start | bytes 1835008 | tf_op jit(solution)/shard_map/all_to_all | solution.py:98
  172.6 113.6 %all-reduce.3.cloned.1.call-start = ((), (), s32[]{:S(2)}) async-start(), calls=%async_computation.9 | async-start | bytes 5308416
  174.8 218.8 %reduce-scatter.3.cloned.1.call-start = ((), (), s32[]{:S(2)}) async-start(), calls=%async_computation.8 | async-start | bytes 8773632 | tf_op jit(solution)/shard_map/reduce_scatter | solution.py:110
  198.6 1.0 copy-start.3
  204.1 0.7 copy-start.12
  204.1 1.9 copy-start.1
  206.0 1.5 copy-start.4
Sparse Core Ops, SparseCore 0:
  10.1 42.0 all-gather.4
  54.5 53.1 all-gather.2
  177.0 109.1 all-reduce.2
  290.6 102.8 reduce-scatter.2
where the time goes:
time: 401 us; the launch traced here: 400 us
  waiting for transfers between devices  310 us (77%)
  matrix products  27.5 us (7%)
  starting transfers between devices  24.8 us (6%)
  local copies, waits for them, and re-layouts  17.5 us (4%)
  between operations  14.7 us (4%)
  other arithmetic  5.81 us (1%)
    reduce_scatter x1, waiting for transfers between devices, per_device(): lax.psum_scatter(part_qkv, 'tm', scatter_dimension=0, tiled=True)  105 us
    unnamed x5, waiting for transfers between devices  74.9 us
    all_gather x1, waiting for transfers between devices, per_device(): lax.all_gather(w_qkv, 'tm', axis=0, tiled=True)  48.6 us
    all_gather x1, waiting for transfers between devices, per_device(): lax.all_gather(w_out, 'tm', axis=0, tiled=True)  33.7 us
    all_to_all x1, waiting for transfers between devices, per_device(): lax.all_to_all(dqkv_cols, 'tm', split_axis=2, concat_axis=2, tiled=True)  23.5 us
    all_to_all x1, waiting for transfers between devices, per_device(): lax.all_to_all(qkv.reshape(videos, per_owner, owners, -1), 'tm', split_ax...  18.1 us
  transfers between devices with their start and end apart: 9, of which 7 were waited for; matrix products, arithmetic and copies ran while one was open for 9% of the time, Pallas kernels for 0%

commit v1 on v0

--- a/solution.py
+++ b/solution.py
@@ -2,12 +2,19 @@
 import jax.numpy as jnp
 from jax import lax
 from jax.sharding import PartitionSpec as P
+from jax.lax import all_to_all, axis_size
 
 HD = 72
 SPLIT = 4
 TB = 2
 TILE = 16
 EPS = 1e-06
+
+
+def field_launch(slab_in):
+    outer = all_to_all(jnp.stack(jnp.split(slab_in, axis_size("tm"), 2), axis=0), "tm", 0, 0)
+    e_now = jnp.concatenate(outer, 2)
+    return e_now
 
 
 def temporal(qkv_cols, dattn_cols, keep_cols, block_mask, frames):
@@ -95,7 +102,7 @@
     attn_cols, dqkv_cols = temporal(qkv_cols, dattn_cols, keep_cols, block_mask, frames)
     attn_rows, dqkv_rows = (
         lax.all_to_all(attn_cols, "tm", split_axis=2, concat_axis=2, tiled=True),
-        lax.all_to_all(dqkv_cols, "tm", split_axis=2, concat_axis=2, tiled=True),
+        field_launch(dqkv_cols),
     )
     attn = attn_rows.reshape(videos, band_len, -1)
     d_qkv = dqkv_rows.reshape(videos, band_len, -1)

time: 401 us -> 406 us (1.012)
  local copies, waits for them, and re-layouts: 17.5 us -> 28.7 us
  waiting for transfers between devices: 310 us -> 305 us
    unnamed x29 -> x42, local copies, waits for them, and re-layouts: 4.9 us -> 14.3 us
    all_to_all x1, waiting for transfers between devices: 5.62 us -> 0.01 us  [per_device(): lax.all_to_all(attn_cols, 'tm', split_axis=2, concat_axis=2, tiled=True)]
  transfers between devices with their start and end apart: 9 -> 9, of which waited for: 7 -> 6; matrix products, arithmetic and copies ran while one was open for 9% -> 11% of each run, Pallas kernels for 0% -> 0%
where the time goes in v1:
time: 406 us; the launch traced here: 405 us
  waiting for transfers between devices  305 us (75%)
  local copies, waits for them, and re-layouts  28.7 us (7%)
  starting transfers between devices  27.3 us (7%)
  matrix products  24.6 us (6%)
  between operations  14.7 us (4%)
  other arithmetic  5.19 us (1%)
    reduce_scatter x1, waiting for transfers between devices, per_device(): lax.psum_scatter(part_qkv, 'tm', scatter_dimension=0, tiled=True)  105 us
    unnamed x5, waiting for transfers between devices  74.9 us
    all_gather x1, waiting for transfers between devices, per_device(): lax.all_gather(w_qkv, 'tm', axis=0, tiled=True)  48.6 us
    all_gather x1, waiting for transfers between devices, per_device(): lax.all_gather(w_out, 'tm', axis=0, tiled=True)  33.7 us
    all_to_all x1, waiting for transfers between devices, field_launch(): all_to_all(jnp.stack(jnp.split(slab_in, axis_size('tm'), 2), axis=0), 'tm...  23.5 us
    all_to_all x1, waiting for transfers between devices, per_device(): lax.all_to_all(qkv.reshape(videos, per_owner, owners, -1), 'tm', split_ax...  18.7 us
    unnamed x42, local copies, waits for them, and re-layouts  14.3 us
  transfers between devices with their start and end apart: 9, of which 6 were waited for; matrix products, arithmetic and copies ran while one was open for 11% of the time, Pallas kernels for 0%

profile of v1, /device:TPU:0, one launch (start us, length us, event | category | flops | bytes accessed | tf_op | source)
XLA Modules:
  0.0 405.2 jit_solution(10789971251307477563)
XLA Ops:
  9.9 7.4 %all-to-all-start.1 = ((s32[1,16,16]{1,0,2:T(1,128)}), s32[1,16,16]{1,0,2:T(1,128)S(1)}, u32[]{:S(2)}, u32[]{:S(2)}) async-start(s32[1,16,16]{1,0,2:T(1,128)} %broadcast_in_dim.16), calls=%async_computation.1 | async-start | bytes 16384 | tf_op jit(solution)/shard_map/all_to_all | solution.py:100
  18.6 33.7 %all-gather.5.cloned.1.call-done = bf16[1152,576]{1,0:T(8,128)(2,1)} async-done(((bf16[72,576]{1,0:T(8,128)(2,1)}), bf16[1152,576]{1,0:T(8,128)(2,1)}) %all-gather.5.cloned.1.call-update) | async-done | bytes 1327120 | tf_op jit(solution)/shard_map/all_gather | solution.py:76
  52.2 2.3 convolution_convert_fusion.4
  55.5 3.5 all-to-all-start.3
  59.1 48.6 %all-gather.3.cloned.1.call-done = bf16[1152,1728]{1,0:T(8,128)(2,1)} async-done(((bf16[72,1728]{1,0:T(8,128)(2,1)}), bf16[1152,1728]{1,0:T(8,128)(2,1)}) %all-gather.3.cloned.1.call-update) | async-done | bytes 3981328 | tf_op jit(solution)/shard_map/all_gather | solution.py:75
  107.7 4.0 convolution_convert_fusion.1
  112.3 1.3 copy.397
  113.6 3.9 all-to-all-start
  118.1 1.4 reshape.297
  119.5 18.7 %all-to-all-done = bf16[1,16,16,1728]{3,1,0,2:T(8,128)(2,1)S(1)} async-done(((bf16[1,16,16,1728]{3,1,0,2:T(8,128)(2,1)}), bf16[1,16,16,1728]{3,1,0,2:T(8,128)(2,1)S(1)}, u32[]{:S(2)}, u32[]{:S(2)}) %all-to-all-start) | async-done | bytes 884768 | tf_op jit(solution)/shard_map/all_to_all | solution.py:86
  138.2 1.7 reshape.296
  141.2 2.0 fusion.36
  145.1 1.4 multiply_reduce_fusion
  150.4 6.1 %all-to-all-start.2 = ((bf16[1,16,16,576]{3,1,0,2:T(8,128)(2,1)}), bf16[1,16,16,576]{3,1,0,2:T(8,128)(2,1)S(1)}, u32[]{:S(2)}, u32[]{:S(2)}) async-start(bf16[1,16,16,576]{3,1,0,2:T(8,128)(2,1)} %reshape.292), calls=%async_computation.2 | async-start | bytes 655360 | tf_op jit(solution)/shard_map/all_to_all | solution.py:104
  156.5 1.5 pad_maximum_fusion
  159.5 1.9 fusion.35
  171.5 6.1 %all-to-all-start.4 = ((bf16[16,1,16,1,1728]{4,2,3,1,0:T(8,128)(2,1)}), bf16[16,1,16,1,1728]{4,2,3,1,0:T(8,128)(2,1)S(1)}, u32[]{:S(2)}, u32[]{:S(2)}) async-start(bf16[16,1,16,1,1728]{4,2,3,1,0:T(8,128)(2,1)} %bitcast_dynamic-update-slice_fusion), calls=%async_computation.4 | async-start | bytes 1835008 | tf_op jit(solution)/shard_map/all_to_all | solution.py:15
  177.8 2.0 convolution_bitcast_fusion
  179.9 23.5 %all-to-all-done.4 = bf16[16,1,16,1,1728]{4,2,3,1,0:T(8,128)(2,1)S(1)} async-done(((bf16[16,1,16,1,1728]{4,2,3,1,0:T(8,128)(2,1)}), bf16[16,1,16,1,1728]{4,2,3,1,0:T(8,128)(2,1)S(1)}, u32[]{:S(2)}, u32[]{:S(2)}) %all-to-all-start.4) | async-done | bytes 884768 | tf_op jit(solution)/shard_map/all_to_all | solution.py:15
  204.7 4.6 %fusion.31 = f32[1152,1728]{1,0:T(8,128)} fusion(bf16[256,1728]{1,0:T(8,128)(2,1)S(1)} %bitcast.134, bf16[1,256,1152]{2,1,0:T(8,128)(2,1)S(1)} %copy-done, f32[1152]{0:T(1024)S(1)} %copy-done.9, f32[256]{0:T(256)S(1)} %add_rsqrt_fusion), kind=kOutput, calls=%fused_computation.51 | convolution fusion | flops 1020395520 | bytes 9442816 | tf_op jit(solution)/shard_map/vtd,vte->de/dot_general | solution.py:109
  211.2 1.5 fusion.2
  212.6 3.6 fusion.3
  217.8 73.5 %all-reduce.3.cloned.1.call-done = f32[1152,576]{0,1:T(8,128)} async-done(((f32[1152,576]{0,1:T(8,128)}), f32[1152,576]{0,1:T(8,128)}) %all-reduce.3.cloned.1.call-update) | async-done | bytes 2654224
  293.3 105.4 %reduce-scatter.3.cloned.1.call-done = f32[72,1728]{1,0:T(8,128)} async-done(((f32[1152,1728]{1,0:T(8,128)}), f32[72,1728]{1,0:T(8,128)}) %reduce-scatter.3.cloned.1.call-update) | async-done | bytes 497680 | tf_op jit(solution)/shard_map/reduce_scatter | solution.py:117
  (86 shorter events, 30.9 us)
Async XLA Ops:
  7.2 45.1 %all-gather.5.cloned.1.call-start = ((), (), s32[]{:S(2)}) async-start(), calls=%async_computation.7 | async-start | bytes 1566720 | tf_op jit(solution)/shard_map/all_gather | solution.py:76
  7.9 99.8 %all-gather.3.cloned.1.call-start = ((), (), s32[]{:S(2)}) async-start(), calls=%async_computation.6 | async-start | bytes 4386816 | tf_op jit(solution)/shard_map/all_gather | solution.py:75
  9.9 45.6 %all-to-all-start.1 = ((s32[1,16,16]{1,0,2:T(1,128)}), s32[1,16,16]{1,0,2:T(1,128)S(1)}, u32[]{:S(2)}, u32[]{:S(2)}) async-start(s32[1,16,16]{1,0,2:T(1,128)} %broadcast_in_dim.16), calls=%async_computation.1 | async-start | bytes 16384 | tf_op jit(solution)/shard_map/all_to_all | solution.py:100
  54.5 53.2 %copy-start = (bf16[1,256,1152]{2,1,0:T(8,128)(2,1)S(1)}, bf16[1,256,1152]{2,1,0:T(8,128)(2,1)}, u32[]{:S(2)}) copy-start(bf16[1,256,1152]{2,1,0:T(8,128)(2,1)} %param.7) | copy-start | bytes 1769476
  54.5 53.2 %copy-start.9 = (f32[1152]{0:T(1024)S(1)}, f32[1152]{0:T(1024)}, u32[]{:S(2)}) copy-start(f32[1152]{0:T(1024)} %param.8) | copy-start | bytes 13828
  55.5 58.1 %all-to-all-start.3 = ((bf16[1,16,16,576]{3,1,0,2:T(8,128)(2,1)}), bf16[1,16,16,576]{3,1,0,2:T(8,128)(2,1)S(1)}, u32[]{:S(2)}, u32[]{:S(2)}) async-start(bf16[1,16,16,576]{3,1,0,2:T(8,128)(2,1)} %copy.410), calls=%async_computation.3 | async-start | bytes 655360 | tf_op jit(solution)/shard_map/all_to_all | solution.py:93
  113.6 4.0 copy-start.10
  113.6 24.5 %all-to-all-start = ((bf16[1,16,16,1728]{3,1,0,2:T(8,128)(2,1)}), bf16[1,16,16,1728]{3,1,0,2:T(8,128)(2,1)S(1)}, u32[]{:S(2)}, u32[]{:S(2)}) async-start(bf16[1,16,16,1728]{3,1,0,2:T(8,128)(2,1)} %copy.397), calls=%async_computation | async-start | bytes 1835008 | tf_op jit(solution)/shard_map/all_to_all | solution.py:86
  141.2 2.0 copy-start.6
  141.2 2.0 copy-start.5
  143.1 1.0 copy-start.8
  146.5 1.0 copy-start.7
  150.4 21.1 %all-to-all-start.2 = ((bf16[1,16,16,576]{3,1,0,2:T(8,128)(2,1)}), bf16[1,16,16,576]{3,1,0,2:T(8,128)(2,1)S(1)}, u32[]{:S(2)}, u32[]{:S(2)}) async-start(bf16[1,16,16,576]{3,1,0,2:T(8,128)(2,1)} %reshape.292), calls=%async_computation.2 | async-start | bytes 655360 | tf_op jit(solution)/shard_map/all_to_all | solution.py:104
  171.5 6.3 %copy-start.2 = (bf16[1,256,1152]{2,1,0:T(8,128)(2,1)S(1)}, bf16[1,256,1152]{2,1,0:T(8,128)(2,1)}, u32[]{:S(2)}) copy-start(bf16[1,256,1152]{2,1,0:T(8,128)(2,1)} %param.13) | copy-start | bytes 1769476
  171.5 31.9 %all-to-all-start.4 = ((bf16[16,1,16,1,1728]{4,2,3,1,0:T(8,128)(2,1)}), bf16[16,1,16,1,1728]{4,2,3,1,0:T(8,128)(2,1)S(1)}, u32[]{:S(2)}, u32[]{:S(2)}) async-start(bf16[16,1,16,1,1728]{4,2,3,1,0:T(8,128)(2,1)} %bitcast_dynamic-update-slice_fusion), calls=%async_computation.4 | async-start | bytes 1835008 | tf_op jit(solution)/shard_map/all_to_all | solution.py:15
  177.7 113.6 %all-reduce.3.cloned.1.call-start = ((), (), s32[]{:S(2)}) async-start(), calls=%async_computation.9 | async-start | bytes 5308416
  179.9 218.8 %reduce-scatter.3.cloned.1.call-start = ((), (), s32[]{:S(2)}) async-start(), calls=%async_computation.8 | async-start | bytes 8773632 | tf_op jit(solution)/shard_map/reduce_scatter | solution.py:117
  203.7 1.0 copy-start.3
  209.3 0.7 copy-start.11
  209.3 1.9 copy-start.1
  211.2 1.5 copy-start.4
Sparse Core Ops, SparseCore 0:
  10.1 42.0 all-gather.4
  54.5 53.1 all-gather.2
  182.1 109.1 all-reduce.2
  295.8 102.8 reduce-scatter.2
